TPU v7x, 32 devices: a whole 2x2x4 slice. The times are simulated.
32 devices in a mesh: gx: 8 (over y, x, core), gy: 4 (over z).
Axes of the slice: x: 2, y: 2, z: 4, core: 2. Of those that a mesh axis runs over, the one named last changes fastest.
Arguments:
- field: float32 [32, 128, 1024], P('gx', 'gy'), may hold values from -6 to 6
- cotangent: float32 [32, 128, 1024], P('gx', 'gy'), may hold values from -6 to 6
- spectral_weight: float32 [32, 32, 2, 32, 512], P('gx', None, None, None, 'gy'), may hold values from -6 to 6
- point_weight: float32 [32, 32], replicated, may hold values from -1 to 1
- point_bias: float32 [32], replicated, may hold values from -3 to 3
Outputs:
- output: float32 [32, 128, 1024], P('gx', 'gy')
- grad_field: float32 [32, 128, 1024], P('gx', 'gy')
- grad_spectral: float32 [32, 32, 2, 32, 512], P('gx', None, None, None, 'gy')
- grad_point: float32 [32, 32], replicated
- grad_bias: float32 [32], replicated
All inputs are finite; a program needn't handle non-finite values.
Results may differ from a plain program's by a relative error of at most 0.00013.
Values sent between devices are 32-bit elements; how exact they have to be, the bound alone decides.
A program may use at most 128 MiB of HBM per device.

v0:
```python
import functools
import math

import jax
import jax.numpy as jnp
import ml_dtypes
import numpy as np
from jax import lax
from jax.experimental import pallas as pl
from jax.experimental.pallas import tpu as pltpu
from jax.sharding import PartitionSpec as P

F32 = jnp.float32
BF16 = jnp.bfloat16
MESH = pl.DeviceIdType.MESH
HIGHEST = lax.Precision.HIGHEST
WIDE = 256
ROWS = 8
VMEM_BYTES = 58 * 1024 * 1024


def phases(positions, length, modes, signed):
    index = np.arange(modes)
    frequency = np.where(index >= modes // 2, index - modes, index) if signed else index
    turns = np.mod(positions[:, None] * frequency[None, :], length) * (2.0 * math.pi / length)
    return np.cos(turns), np.sin(turns)


def halves(table):
    table = np.asarray(table, np.float32)
    high = table.astype(ml_dtypes.bfloat16)
    low = (table - high.astype(np.float32)).astype(ml_dtypes.bfloat16)
    return high, low


def thirds(table):
    high, low = halves(table)
    return np.concatenate([high, high, low], -1)


def tables(nx, ny, nz, kx, ky, kz, chan, owned, split_y):
    cos_z, sin_z = phases(np.arange(nz), nz, kz, False)
    eye = np.eye(chan)
    first = np.concatenate([np.kron(cos_z, eye), np.kron(-sin_z, eye)], 1)
    cos_y, sin_y = phases(np.arange(ny), ny, ky, True)
    cells = ny // split_y
    cos_y = cos_y.reshape(split_y, cells, ky).transpose(0, 2, 1)
    sin_y = sin_y.reshape(split_y, cells, ky).transpose(0, 2, 1)
    real = np.concatenate([cos_y, sin_y], 2)
    imag = np.concatenate([-sin_y, cos_y], 2)
    second = np.stack([real, imag], 2).reshape(split_y, 2 * ky, 2 * cells)
    cos_x, sin_x = phases(np.arange(nx), nx, kx, True)
    third = np.zeros((owned, 2, kx, nx, owned, 2))
    for q in range(owned):
        third[q, 0, :, :, q, 0] = cos_x.T
        third[q, 0, :, :, q, 1] = sin_x.T
        third[q, 1, :, :, q, 0] = -sin_x.T
        third[q, 1, :, :, q, 1] = cos_x.T
    third = third.reshape(owned * 2 * kx, nx * owned * 2)
    return (
        *halves(first),
        *halves(first.T),
        thirds(second),
        thirds(second.transpose(0, 2, 1)),
        *halves(third),
        *halves(third.T),
    )


def parts_of(value):
    high = value.astype(BF16)
    return high, (value - high.astype(F32)).astype(BF16)


def dot(left, right):
    return jnp.dot(left, right, preferred_element_type=F32)


def right_product(value, high_table, low_table):
    rows = value.shape[0]
    high, low = parts_of(value)
    both = dot(jnp.concatenate([high, low], 0), high_table)
    return both[:rows] + both[rows:] + dot(high, low_table)


def left_product(high_table, low_table, value):
    columns = value.shape[1]
    high, low = parts_of(value)
    both = dot(high_table, jnp.concatenate([high, low], 1))
    return both[:, :columns] + both[:, columns:] + dot(low_table, high)


def left_thirds(table, value):
    high, low = parts_of(value)
    return dot(table, jnp.concatenate([high, low, high], 0))


def exact(left, right, dims):
    return lax.dot_general(
        left, right, (dims, ((), ())), precision=HIGHEST, preferred_element_type=F32
    )


def iota(shape, axis):
    return lax.broadcasted_iota(jnp.int32, shape, axis)


def kernel(
    sizes,
    field, cotangent, weight_in, point, bias,
    za_high, za_low, zs_high_in, zs_low_in, ya, ys, xa_high, xa_low, xs_high, xs_low,
    output, grad_field, grad_weight_out, grad_point, grad_bias,
    weight, zs_high, zs_low, spread_real, spread_imag, grad_weight, hidden_base, grad_hidden,
    coefficients, mixed,
    rs_out, rs_in, xy_out, xy_in, yx_out, yx_in, gathered, total_y, total_x,
    rs_ss, rs_rs, xy_ss, xy_rs, yx_ss, yx_rs, ag_ss, ag_rs, ty_ss, ty_rs, tx_ss, tx_rs, local_sem, out_sem,
):
    A, B, CX, CY, KX, KC, L, C, owned, cells, steps = sizes
    R2 = 2 * owned
    a = lax.axis_index("gx")
    b = lax.axis_index("gy")

    def peer_x(d):
        return lax.rem(a + d, A)

    def peer_y(d):
        return lax.rem(b + d, B)

    def place(gx, gy):
        return {"gx": gx, "gy": gy}

    def remote(src, dst, ss, rs, where):
        return pltpu.make_async_remote_copy(
            src_ref=src, dst_ref=dst, send_sem=ss, recv_sem=rs, device_id=where, device_id_type=MESH
        )

    barrier = pltpu.get_barrier_semaphore()
    for d in range(1, A):
        pl.semaphore_signal(barrier, inc=1, device_id=place(peer_x(d), b), device_id_type=MESH)
    for d in range(1, B):
        pl.semaphore_signal(barrier, inc=1, device_id=place(a, peer_y(d)), device_id_type=MESH)
    loads = [
        pltpu.make_async_copy(weight_in, weight, local_sem.at[0]),
        pltpu.make_async_copy(zs_high_in, zs_high, local_sem.at[1]),
        pltpu.make_async_copy(zs_low_in, zs_low, local_sem.at[2]),
    ]
    for load in loads:
        load.start()
    sends = []

    def analyse_columns(turn, rows, first):
        z = right_product(rows, za_high[...], za_low[...])
        for n in range(rows.shape[0] // CY):
            one = z[n * CY : (n + 1) * CY]
            y = left_thirds(ya[b], jnp.concatenate([one[:, :KC], one[:, KC:]], 0))
            for j in range(B):
                rs_out[turn, j, first + n] = y[:, j * L : (j + 1) * L]

    def scatter(turn, x):
        made = []
        for d in range(1, B):
            copy = remote(
                rs_out.at[turn, peer_y(d), x], rs_in.at[turn, d, x],
                rs_ss.at[turn, d, x], rs_rs.at[turn, d, x], place(a, peer_y(d)),
            )
            copy.start()
            made.append(copy)
        sends.extend(made)
        return made

    def sum_and_send(turn, first, count, arriving):
        for n in range(count):
            x = first + n
            total = rs_out[turn, b, x]
            for d, copy in enumerate(arriving[x], 1):
                copy.wait_recv()
                total = total + rs_in[turn, d, x]
            for s in range(A):
                xy_out[turn, s, x] = total[s * R2 : (s + 1) * R2]
        h = first // count
        made = []
        for d in range(1, A):
            copy = remote(
                xy_out.at[turn, peer_x(d), pl.ds(first, count)], xy_in.at[turn, a, pl.ds(first, count)],
                xy_ss.at[turn, d, h], xy_rs.at[turn, d, h], place(peer_x(d), b),
            )
            copy.start()
            made.append(copy)
        sends.extend(made)
        xy_in[turn, a, pl.ds(first, count)] = xy_out[turn, a, pl.ds(first, count)]
        return made

    def transform_x(turn, arriving):
        for copy in arriving:
            copy.wait_recv()
        if R2 % ROWS == 0:
            value = xy_in[turn].reshape(A * CX * R2, L)
        else:
            value = jnp.concatenate([xy_in[turn, s, x] for s in range(A) for x in range(CX)], 0)
        return left_product(xa_high[...], xa_low[...], value)

    def back_x(turn):
        value = left_product(xs_high[...], xs_low[...], mixed[...])
        for s in range(A):
            for x in range(CX):
                at = (s * CX + x) * R2
                yx_out[turn, s, x] = value[at : at + R2]
        made = []
        for d in range(1, A):
            copy = remote(
                yx_out.at[turn, peer_x(d)], yx_in.at[turn, a],
                yx_ss.at[turn, d], yx_rs.at[turn, d], place(peer_x(d), b),
            )
            copy.start()
            made.append(copy)
        sends.extend(made)
        yx_in[turn, a] = yx_out[turn, a]
        return made

    def gather(turn, arriving):
        for copy in arriving:
            copy.wait_recv()
        made = []
        count = CX // steps
        for h in range(steps):
            for x in range(h * count, (h + 1) * count):
                for s in range(A):
                    gathered[turn, b, x, s * R2 : (s + 1) * R2] = yx_in[turn, s, x]
            own = gathered.at[turn, b, pl.ds(h * count, count)]
            group = []
            for d in range(1, B):
                copy = remote(
                    own, own, ag_ss.at[turn, d, h], ag_rs.at[turn, d, h], place(a, peer_y(d))
                )
                copy.start()
                group.append(copy)
            sends.extend(group)
            made.append(group)
        return made

    def synthesise_columns(turn, first, count, arriving):
        for copy in arriving:
            copy.wait_recv()
        slabs = []
        for x in range(first, first + count):
            modes = jnp.concatenate([gathered[turn, j, x] for j in range(B)], 1)
            grid = left_thirds(ys[b], modes)
            slabs.append(jnp.concatenate([grid[:CY], grid[CY:]], 1))
        return right_product(jnp.concatenate(slabs, 0), zs_high[...], zs_low[...])

    fold = (iota((WIDE, C), 0) % C == iota((WIDE, C), 1)).astype(F32)
    fold_wide = (iota((WIDE, L), 0) % C == iota((WIDE, L), 1)).astype(F32)
    same = (iota((WIDE, WIDE), 0) // C == iota((WIDE, WIDE), 1) // C).astype(F32)
    pick = (iota((C, L), 0) == iota((C, L), 1) % C).astype(F32)
    group = ((iota((2 * L, L), 0) % L) // C == iota((2 * L, L), 1) // C).astype(F32).astype(BF16)
    mode = b * (L // C) + iota((1, L), 1) // C
    factor = jnp.where(mode == 0, 1.0, 2.0).astype(F32) * (1.0 / cells)
    columns = field.shape[2]
    blocks = columns // WIDE

    def stacked(value):
        return jnp.concatenate([value[:, j * WIDE : (j + 1) * WIDE] for j in range(blocks)], 0)

    def unstacked(value):
        rows = value.shape[0] // blocks
        return jnp.concatenate([value[j * rows : (j + 1) * rows] for j in range(blocks)], 1)

    def pointwise(value, axis):
        table = exact(exact(fold, point[...], ((1,), (axis,))), fold, ((1,), (1,))) * same
        return unstacked(right_product(stacked(value), *parts_of(table)))

    signal = field[...].reshape(CX * CY, columns)
    analyse_columns(0, signal, 0)
    pl.semaphore_wait(barrier, A + B - 2)
    arriving = [scatter(0, x) for x in range(CX)]
    tiled = exact(bias[...], fold, ((1,), (1,)))
    hidden_base[...] = pointwise(signal, 0) + jnp.concatenate([tiled] * blocks, 1)
    count = CX // steps
    moved = []
    for h in range(steps):
        moved += sum_and_send(0, h * count, count, arriving)
    coefficients[...] = transform_x(0, moved)
    loads[0].wait()
    per = KX // ROWS

    def place_of(t):
        q = t // per
        p = (t % per) * ROWS
        return q, p, pl.multiple_of(q * (2 * KX) + p, ROWS)

    def grouped(high, low):
        return dot(jnp.concatenate([high, low], 1), group)

    def widen(value):
        high, low = parts_of(value)
        pair = [
            (part.astype(F32)[:, None, :] * pick[None]).reshape(ROWS * C, L).astype(BF16)
            for part in (high, low)
        ]
        return grouped(*pair).reshape(ROWS, C, L)

    def mix(t, carry):
        q, p, at = place_of(t)
        real = widen(coefficients[pl.ds(at, ROWS)])
        imag = widen(coefficients[pl.ds(at + KX, ROWS)])
        spread_real[q, pl.ds(p, ROWS)] = real
        spread_imag[q, pl.ds(p, ROWS)] = imag
        w_real = weight[q, pl.ds(p, ROWS), 0]
        w_imag = weight[q, pl.ds(p, ROWS), 1]
        mixed[pl.ds(at, ROWS)] = jnp.sum(real * w_real - imag * w_imag, 1) * factor
        mixed[pl.ds(at + KX, ROWS)] = jnp.sum(real * w_imag + imag * w_real, 1) * factor
        return carry

    lax.fori_loop(0, owned * per, mix, 0)
    returned = gather(0, back_x(0))
    loads[1].wait()
    loads[2].wait()

    arriving = []
    for h in range(steps):
        rows = count * CY
        at = h * rows
        value = synthesise_columns(0, h * count, count, returned[h]) + hidden_base[at : at + rows]
        below = 0.5 * (1.0 + lax.erf(value * math.sqrt(0.5)))
        density = jnp.exp(-0.5 * value * value) * (1.0 / math.sqrt(2.0 * math.pi))
        output[h * count : (h + 1) * count] = (value * below).reshape(count, CY, columns)
        upper = cotangent[h * count : (h + 1) * count].reshape(rows, columns)
        slope = upper * (below + value * density)
        grad_hidden[at : at + rows] = slope
        analyse_columns(1, slope, h * count)
        arriving += [scatter(1, h * count + n) for n in range(count)]

    slope = grad_hidden[...]
    left = parts_of(stacked(field[...].reshape(CX * CY, columns)))
    right = parts_of(stacked(slope))

    def crossed(one, two):
        return lax.dot_general(one, two, (((0,), (0,)), ((), ())), preferred_element_type=F32)

    pairs = (crossed(left[0], right[0]) + crossed(left[0], right[1]) + crossed(left[1], right[0])) * same
    point_part = exact(exact(fold, pairs, ((0,), (0,))), fold_wide, ((1,), (0,)))
    bias_part = exact(jnp.sum(stacked(slope), 0, keepdims=True), fold_wide, ((1,), (0,)))
    total_y[b, 0:C] = point_part
    total_y[b, C : C + ROWS] = jnp.broadcast_to(bias_part, (ROWS, L))
    own = total_y.at[b]
    totals = []
    for d in range(1, B):
        copy = remote(own, own, ty_ss.at[d], ty_rs.at[d], place(a, peer_y(d)))
        copy.start()
        totals.append(copy)
    sends.extend(totals)
    hidden_base[...] = pointwise(slope, 1)

    moved = []
    for h in range(steps):
        moved += sum_and_send(1, h * count, count, arriving)
    for copy in totals:
        copy.wait_recv()
    total = total_y[0]
    for j in range(1, B):
        total = total + total_y[j]
    total_x[a] = total
    own = total_x.at[a]
    totals = []
    for d in range(1, A):
        copy = remote(own, own, tx_ss.at[d], tx_rs.at[d], place(peer_x(d), b))
        copy.start()
        totals.append(copy)
    sends.extend(totals)
    coefficients[...] = transform_x(1, moved) * factor

    def unmix(t, carry):
        q, p, at = place_of(t)
        real = coefficients[pl.ds(at, ROWS)][:, None, :]
        imag = coefficients[pl.ds(at + KX, ROWS)][:, None, :]
        w_real = weight[q, pl.ds(p, ROWS), 0]
        w_imag = weight[q, pl.ds(p, ROWS), 1]
        for term, to in ((real * w_real + imag * w_imag, at), (imag * w_real - real * w_imag, at + KX)):
            summed = grouped(*parts_of(term.reshape(ROWS * C, L))).reshape(ROWS, C, L)
            mixed[pl.ds(to, ROWS)] = jnp.sum(summed * pick[None], 1)
        return carry

    lax.fori_loop(0, owned * per, unmix, 0)
    back = back_x(1)

    def weigh(t, carry):
        q, p, at = place_of(t)
        real = coefficients[pl.ds(at, ROWS)][:, None, :]
        imag = coefficients[pl.ds(at + KX, ROWS)][:, None, :]
        s_real = spread_real[q, pl.ds(p, ROWS)]
        s_imag = spread_imag[q, pl.ds(p, ROWS)]
        grad_weight[q, pl.ds(p, ROWS), 0] = s_real * real + s_imag * imag
        grad_weight[q, pl.ds(p, ROWS), 1] = s_real * imag - s_imag * real
        return carry

    returned = gather(1, back)
    lax.fori_loop(0, owned * per, weigh, 0)
    store = pltpu.make_async_copy(grad_weight, grad_weight_out, out_sem.at[0])
    store.start()
    for copy in totals:
        copy.wait_recv()
    total = total_x[0]
    for s in range(1, A):
        total = total + total_x[s]
    total = total * (1.0 / math.sqrt(cells))
    grad_point[...] = total[0:C, 0:C]
    grad_bias[...] = total[C : C + 1, 0:C]
    for h in range(steps):
        rows = count * CY
        at = h * rows
        value = synthesise_columns(1, h * count, count, returned[h]) + hidden_base[at : at + rows]
        grad_field[h * count : (h + 1) * count] = value.reshape(count, CY, columns)
    store.wait()
    for copy in sends:
        copy.wait_send()


def shards(A, B, field, cotangent, weight, point, bias):
    CX, CY, columns = field.shape
    C = point.shape[0]
    owned, KX, _, _, L = weight.shape
    depth = L // C
    KY, KZ, NZ = owned * A, depth * B, columns // C
    NX, NY = CX * A, CY * B
    cells = NX * NY * NZ
    R, R2, KC = 2 * KY, 2 * owned, KZ * C
    steps = 2 if CX % 2 == 0 else 1
    made = [jnp.asarray(t) for t in tables(NX, NY, NZ, KX, KY, KZ, C, owned, B)]
    sizes = (A, B, CX, CY, KX, KC, L, C, owned, cells, steps)
    vmem = pl.BlockSpec(memory_space=pltpu.VMEM)
    far = pl.BlockSpec(memory_space=pl.ANY)
    dma = pltpu.SemaphoreType.DMA
    z_shape = made[2].shape
    modes = owned * 2 * KX
    results = pl.pallas_call(
        functools.partial(kernel, sizes),
        out_shape=(
            jax.ShapeDtypeStruct(field.shape, F32),
            jax.ShapeDtypeStruct(field.shape, F32),
            jax.ShapeDtypeStruct(weight.shape, F32),
            jax.ShapeDtypeStruct((C, C), F32),
            jax.ShapeDtypeStruct((1, C), F32),
        ),
        in_specs=[vmem, vmem, far, vmem, vmem, vmem, vmem, far, far] + [vmem] * 6,
        out_specs=(vmem, vmem, far, vmem, vmem),
        scratch_shapes=[
            pltpu.VMEM(weight.shape, F32),
            pltpu.VMEM(z_shape, BF16),
            pltpu.VMEM(z_shape, BF16),
            pltpu.VMEM((owned, KX, C, L), F32),
            pltpu.VMEM((owned, KX, C, L), F32),
            pltpu.VMEM(weight.shape, F32),
            pltpu.VMEM((CX * CY, columns), F32),
            pltpu.VMEM((CX * CY, columns), F32),
            pltpu.VMEM((modes, L), F32),
            pltpu.VMEM((modes, L), F32),
            pltpu.VMEM((2, B, CX, R, L), F32),
            pltpu.VMEM((2, B, CX, R, L), F32),
            pltpu.VMEM((2, A, CX, R2, L), F32),
            pltpu.VMEM((2, A, CX, R2, L), F32),
            pltpu.VMEM((2, A, CX, R2, L), F32),
            pltpu.VMEM((2, A, CX, R2, L), F32),
            pltpu.VMEM((2, B, CX, R, L), F32),
            pltpu.VMEM((B, C + ROWS, L), F32),
            pltpu.VMEM((A, C + ROWS, L), F32),
            dma((2, B, CX)), dma((2, B, CX)),
            dma((2, A, steps)), dma((2, A, steps)),
            dma((2, A)), dma((2, A)),
            dma((2, B, steps)), dma((2, B, steps)),
            dma((B,)), dma((B,)),
            dma((A,)), dma((A,)),
            dma((3,)), dma((1,)),
        ],
        compiler_params=pltpu.CompilerParams(
            collective_id=0, has_side_effects=True, vmem_limit_bytes=VMEM_BYTES
        ),
    )(field, cotangent, weight, point, bias.reshape(1, C), *made)
    return (*results[:4], results[4].reshape(C))


def solution(mesh):
    placed = (P("gx", "gy", None), P("gx", "gy", None), P("gx", None, None, None, "gy"), P(), P())
    return jax.shard_map(
        functools.partial(shards, mesh.shape["gx"], mesh.shape["gy"]),
        mesh=mesh,
        in_specs=placed,
        out_specs=(
            P("gx", "gy", None),
            P("gx", "gy", None),
            P("gx", None, None, None, "gy"),
            P(),
            P(),
        ),
        check_vma=False,
    )
```

profile of v0, /device:TPU:0, one launch (start us, length us, event | category | flops | bytes accessed | tf_op | source)
XLA Modules:
  0.0 95.9 jit_solution(11447161910454631272)
XLA Ops:
  0.6 85.4 %shard_map.182 = (f32[4,32,1024]{2,1,0:T(8,128)}, f32[4,32,1024]{2,1,0:T(8,128)}, f32[4,32,2,32,128]{4,3,2,1,0:T(8,128)}, f32[32,32]{1,0:T(8,128)}, f32[1,32]{1,0:T(1,128)}) custom-call(f32[4,32,1024]{2,1,0:T(8,128)} %field.1, f32[4,32,1024]{2,1,0:T(8,128)} %cotangent.1, f32[4,32,2,32,128]{4,3,2,1,0:T(8,128)} %weight_in.1, f32[32,32]{1,0:T(8,128)} %point.1, ...), custom_call_target="tpu_custom_call" | custom-call | tf_op jit(solution)/shard_map/pallas_call | solution.py:435
  86.0 1.9 %copy.25 = f32[4,32,1024]{2,1,0:T(8,128)} copy(f32[4,32,1024]{2,1,0:T(8,128)} %get-tuple-element.20) | data formatting | bytes 1048576
  87.9 1.9 %copy.26 = f32[4,32,1024]{2,1,0:T(8,128)} copy(f32[4,32,1024]{2,1,0:T(8,128)} %get-tuple-element.21) | data formatting | bytes 1048576
  89.8 0.0 copy-start
  89.8 0.0 copy-start.1
  89.8 5.1 %copy.27 = f32[4,32,2,32,128]{4,3,2,1,0:T(8,128)} copy(f32[4,32,2,32,128]{4,3,2,1,0:T(8,128)} %get-tuple-element.22) | data formatting | bytes 8388608
  94.8 0.0 copy-done
  94.8 0.6 copy.28
  95.4 0.0 copy-done.1
  95.4 0.5 copy.29
Async XLA Ops:
  89.8 5.1 %copy-start = (f32[32,32]{1,0:T(8,128)S(1)}, f32[32,32]{1,0:T(8,128)}, u32[]{:S(2)}) copy-start(f32[32,32]{1,0:T(8,128)} %get-tuple-element.23) | copy-start | bytes 12292
  89.8 5.7 %copy-start.1 = (f32[1,32]{1,0:T(1,128)S(1)}, f32[1,32]{1,0:T(1,128)}, u32[]{:S(2)}) copy-start(f32[1,32]{1,0:T(1,128)} %get-tuple-element.14) | copy-start | bytes 388
where the time goes:
time: 96.2 us; the launch traced here: 95.9 us
  Pallas kernels  85.4 us (89%)
  local copies, waits for them, and re-layouts  9.95 us (10%)
    pallas_call x1, Pallas kernels, shards(): pl.pallas_call(functools.partial(kernel, sizes), out_shape=(jax.ShapeDtyp...  85.4 us
    unnamed x9, local copies, waits for them, and re-layouts  9.95 us

commit v1 on v0

--- a/solution.py
+++ b/solution.py
@@ -105,15 +105,64 @@
     return lax.broadcasted_iota(jnp.int32, shape, axis)
 
 
+def channel_tables(C, L):
+    pick = (iota((C, L), 0) == iota((C, L), 1) % C).astype(F32)
+    group = ((iota((2 * L, L), 0) % L) // C == iota((2 * L, L), 1) // C).astype(F32).astype(BF16)
+    return pick, group
+
+
+def grouped(high, low, group):
+    return dot(jnp.concatenate([high, low], 1), group)
+
+
+def widen(value, pick, group):
+    C, L = pick.shape
+    high, low = parts_of(value)
+    pair = [
+        (part.astype(F32)[:, None, :] * pick[None]).reshape(value.shape[0] * C, L).astype(BF16)
+        for part in (high, low)
+    ]
+    return grouped(*pair, group).reshape(value.shape[0], C, L)
+
+
+def finish(
+    sizes, spectrum, slopes, output_in, field_in, point_in, bias_in,
+    output, grad_field, grad_weight_out, grad_point, grad_bias, grad_weight, sem,
+):
+    owned, KX, C, L = sizes
+    copies = [
+        pltpu.make_async_copy(output_in, output, sem.at[owned]),
+        pltpu.make_async_copy(field_in, grad_field, sem.at[owned + 1]),
+    ]
+    for copy in copies:
+        copy.start()
+    grad_point[...] = point_in[...]
+    grad_bias[...] = bias_in[...]
+    pick, group = channel_tables(C, L)
+    for q in range(owned):
+        for p in range(0, KX, ROWS):
+            at = q * 2 * KX + p
+            s_real = widen(spectrum[at : at + ROWS], pick, group)
+            s_imag = widen(spectrum[at + KX : at + KX + ROWS], pick, group)
+            real = slopes[at : at + ROWS][:, None, :]
+            imag = slopes[at + KX : at + KX + ROWS][:, None, :]
+            grad_weight[q, p : p + ROWS, 0] = s_real * real + s_imag * imag
+            grad_weight[q, p : p + ROWS, 1] = s_real * imag - s_imag * real
+        copy = pltpu.make_async_copy(grad_weight.at[q], grad_weight_out.at[q], sem.at[q])
+        copy.start()
+        copies.append(copy)
+    for copy in copies:
+        copy.wait()
+
+
 def kernel(
     sizes,
     field, cotangent, weight_in, point, bias,
     za_high, za_low, zs_high_in, zs_low_in, ya, ys, xa_high, xa_low, xs_high, xs_low,
-    output, grad_field, grad_weight_out, grad_point, grad_bias,
-    weight, zs_high, zs_low, spread_real, spread_imag, grad_weight, hidden_base, grad_hidden,
-    coefficients, mixed,
+    output, grad_field, spectrum, slopes, grad_point, grad_bias,
+    weight, zs_high, zs_low, hidden_base, grad_hidden, mixed,
     rs_out, rs_in, xy_out, xy_in, yx_out, yx_in, gathered, total_y, total_x,
-    rs_ss, rs_rs, xy_ss, xy_rs, yx_ss, yx_rs, ag_ss, ag_rs, ty_ss, ty_rs, tx_ss, tx_rs, local_sem, out_sem,
+    rs_ss, rs_rs, xy_ss, xy_rs, yx_ss, yx_rs, ag_ss, ag_rs, ty_ss, ty_rs, tx_ss, tx_rs, local_sem,
 ):
     A, B, CX, CY, KX, KC, L, C, owned, cells, steps = sizes
     R2 = 2 * owned
@@ -251,8 +300,7 @@
     fold = (iota((WIDE, C), 0) % C == iota((WIDE, C), 1)).astype(F32)
     fold_wide = (iota((WIDE, L), 0) % C == iota((WIDE, L), 1)).astype(F32)
     same = (iota((WIDE, WIDE), 0) // C == iota((WIDE, WIDE), 1) // C).astype(F32)
-    pick = (iota((C, L), 0) == iota((C, L), 1) % C).astype(F32)
-    group = ((iota((2 * L, L), 0) % L) // C == iota((2 * L, L), 1) // C).astype(F32).astype(BF16)
+    pick, group = channel_tables(C, L)
     mode = b * (L // C) + iota((1, L), 1) // C
     factor = jnp.where(mode == 0, 1.0, 2.0).astype(F32) * (1.0 / cells)
     columns = field.shape[2]
@@ -270,16 +318,20 @@
         return unstacked(right_product(stacked(value), *parts_of(table)))
 
     signal = field[...].reshape(CX * CY, columns)
-    analyse_columns(0, signal, 0)
-    pl.semaphore_wait(barrier, A + B - 2)
-    arriving = [scatter(0, x) for x in range(CX)]
+    count = CX // steps
+    rows = count * CY
+    arriving = []
+    for h in range(steps):
+        analyse_columns(0, signal[h * rows : (h + 1) * rows], h * count)
+        if h == 0:
+            pl.semaphore_wait(barrier, A + B - 2)
+        arriving += [scatter(0, h * count + n) for n in range(count)]
     tiled = exact(bias[...], fold, ((1,), (1,)))
     hidden_base[...] = pointwise(signal, 0) + jnp.concatenate([tiled] * blocks, 1)
-    count = CX // steps
     moved = []
     for h in range(steps):
         moved += sum_and_send(0, h * count, count, arriving)
-    coefficients[...] = transform_x(0, moved)
+    spectrum[...] = transform_x(0, moved)
     loads[0].wait()
     per = KX // ROWS
 
@@ -288,30 +340,26 @@
         p = (t % per) * ROWS
         return q, p, pl.multiple_of(q * (2 * KX) + p, ROWS)
 
-    def grouped(high, low):
-        return dot(jnp.concatenate([high, low], 1), group)
-
-    def widen(value):
-        high, low = parts_of(value)
-        pair = [
-            (part.astype(F32)[:, None, :] * pick[None]).reshape(ROWS * C, L).astype(BF16)
-            for part in (high, low)
-        ]
-        return grouped(*pair).reshape(ROWS, C, L)
-
-    def mix(t, carry):
+    def over_modes(step):
+        many = max(n for n in (4, 2, 1) if (owned * per) % n == 0)
+
+        def some(t, carry):
+            for n in range(many):
+                step(t * many + n)
+            return carry
+
+        lax.fori_loop(0, owned * per // many, some, 0)
+
+    def mix(t):
         q, p, at = place_of(t)
-        real = widen(coefficients[pl.ds(at, ROWS)])
-        imag = widen(coefficients[pl.ds(at + KX, ROWS)])
-        spread_real[q, pl.ds(p, ROWS)] = real
-        spread_imag[q, pl.ds(p, ROWS)] = imag
+        real = widen(spectrum[pl.ds(at, ROWS)], pick, group)
+        imag = widen(spectrum[pl.ds(at + KX, ROWS)], pick, group)
         w_real = weight[q, pl.ds(p, ROWS), 0]
         w_imag = weight[q, pl.ds(p, ROWS), 1]
         mixed[pl.ds(at, ROWS)] = jnp.sum(real * w_real - imag * w_imag, 1) * factor
         mixed[pl.ds(at + KX, ROWS)] = jnp.sum(real * w_imag + imag * w_real, 1) * factor
-        return carry
-
-    lax.fori_loop(0, owned * per, mix, 0)
+
+    over_modes(mix)
     returned = gather(0, back_x(0))
     loads[1].wait()
     loads[2].wait()
@@ -367,36 +415,20 @@
         copy.start()
         totals.append(copy)
     sends.extend(totals)
-    coefficients[...] = transform_x(1, moved) * factor
-
-    def unmix(t, carry):
+    slopes[...] = transform_x(1, moved) * factor
+
+    def unmix(t):
         q, p, at = place_of(t)
-        real = coefficients[pl.ds(at, ROWS)][:, None, :]
-        imag = coefficients[pl.ds(at + KX, ROWS)][:, None, :]
+        real = slopes[pl.ds(at, ROWS)][:, None, :]
+        imag = slopes[pl.ds(at + KX, ROWS)][:, None, :]
         w_real = weight[q, pl.ds(p, ROWS), 0]
         w_imag = weight[q, pl.ds(p, ROWS), 1]
         for term, to in ((real * w_real + imag * w_imag, at), (imag * w_real - real * w_imag, at + KX)):
-            summed = grouped(*parts_of(term.reshape(ROWS * C, L))).reshape(ROWS, C, L)
+            summed = grouped(*parts_of(term.reshape(ROWS * C, L)), group).reshape(ROWS, C, L)
             mixed[pl.ds(to, ROWS)] = jnp.sum(summed * pick[None], 1)
-        return carry
-
-    lax.fori_loop(0, owned * per, unmix, 0)
-    back = back_x(1)
-
-    def weigh(t, carry):
-        q, p, at = place_of(t)
-        real = coefficients[pl.ds(at, ROWS)][:, None, :]
-        imag = coefficients[pl.ds(at + KX, ROWS)][:, None, :]
-        s_real = spread_real[q, pl.ds(p, ROWS)]
-        s_imag = spread_imag[q, pl.ds(p, ROWS)]
-        grad_weight[q, pl.ds(p, ROWS), 0] = s_real * real + s_imag * imag
-        grad_weight[q, pl.ds(p, ROWS), 1] = s_real * imag - s_imag * real
-        return carry
-
-    returned = gather(1, back)
-    lax.fori_loop(0, owned * per, weigh, 0)
-    store = pltpu.make_async_copy(grad_weight, grad_weight_out, out_sem.at[0])
-    store.start()
+
+    over_modes(unmix)
+    returned = gather(1, back_x(1))
     for copy in totals:
         copy.wait_recv()
     total = total_x[0]
@@ -410,7 +442,6 @@
         at = h * rows
         value = synthesise_columns(1, h * count, count, returned[h]) + hidden_base[at : at + rows]
         grad_field[h * count : (h + 1) * count] = value.reshape(count, CY, columns)
-    store.wait()
     for copy in sends:
         copy.wait_send()
 
@@ -432,27 +463,24 @@
     dma = pltpu.SemaphoreType.DMA
     z_shape = made[2].shape
     modes = owned * 2 * KX
-    results = pl.pallas_call(
+    output, grad_field, spectrum, slopes, grad_point, grad_bias = pl.pallas_call(
         functools.partial(kernel, sizes),
         out_shape=(
             jax.ShapeDtypeStruct(field.shape, F32),
             jax.ShapeDtypeStruct(field.shape, F32),
-            jax.ShapeDtypeStruct(weight.shape, F32),
+            jax.ShapeDtypeStruct((modes, L), F32),
+            jax.ShapeDtypeStruct((modes, L), F32),
             jax.ShapeDtypeStruct((C, C), F32),
             jax.ShapeDtypeStruct((1, C), F32),
         ),
         in_specs=[vmem, vmem, far, vmem, vmem, vmem, vmem, far, far] + [vmem] * 6,
-        out_specs=(vmem, vmem, far, vmem, vmem),
+        out_specs=(vmem,) * 6,
         scratch_shapes=[
             pltpu.VMEM(weight.shape, F32),
             pltpu.VMEM(z_shape, BF16),
             pltpu.VMEM(z_shape, BF16),
-            pltpu.VMEM((owned, KX, C, L), F32),
-            pltpu.VMEM((owned, KX, C, L), F32),
-            pltpu.VMEM(weight.shape, F32),
             pltpu.VMEM((CX * CY, columns), F32),
             pltpu.VMEM((CX * CY, columns), F32),
-            pltpu.VMEM((modes, L), F32),
             pltpu.VMEM((modes, L), F32),
             pltpu.VMEM((2, B, CX, R, L), F32),
             pltpu.VMEM((2, B, CX, R, L), F32),
@@ -469,12 +497,26 @@
             dma((2, B, steps)), dma((2, B, steps)),
             dma((B,)), dma((B,)),
             dma((A,)), dma((A,)),
-            dma((3,)), dma((1,)),
+            dma((3,)),
         ],
         compiler_params=pltpu.CompilerParams(
             collective_id=0, has_side_effects=True, vmem_limit_bytes=VMEM_BYTES
         ),
     )(field, cotangent, weight, point, bias.reshape(1, C), *made)
+    results = pl.pallas_call(
+        functools.partial(finish, (owned, KX, C, L)),
+        out_shape=(
+            jax.ShapeDtypeStruct(field.shape, F32),
+            jax.ShapeDtypeStruct(field.shape, F32),
+            jax.ShapeDtypeStruct(weight.shape, F32),
+            jax.ShapeDtypeStruct((C, C), F32),
+            jax.ShapeDtypeStruct((1, C), F32),
+        ),
+        in_specs=[vmem, vmem, far, far, vmem, vmem],
+        out_specs=(far, far, far, vmem, vmem),
+        scratch_shapes=[pltpu.VMEM(weight.shape, F32), dma((owned + 2,))],
+        compiler_params=pltpu.CompilerParams(vmem_limit_bytes=VMEM_BYTES),
+    )(spectrum, slopes, output, grad_field, grad_point, grad_bias)
     return (*results[:4], results[4].reshape(C))
 
 

time: 96.2 us -> 117 us (1.22)
  Pallas kernels: 85.4 us -> 116 us
  local copies, waits for them, and re-layouts: 9.95 us -> 0 us
    pallas_call x0 -> x1, Pallas kernels: none -> 34.5 us  [shards(): pl.pallas_call(functools.partial(finish, (owned, KX, C, L)), out_shape=(j...]
    unnamed x9 -> x0, local copies, waits for them, and re-layouts: 9.95 us -> none
    pallas_call x1, Pallas kernels: 85.4 us -> 81.8 us  [shards(): pl.pallas_call(functools.partial(kernel, sizes), out_shape=(jax.ShapeDtyp...]
where the time goes in v1:
time: 117 us
  Pallas kernels  116 us (99%)
    pallas_call x1, Pallas kernels, shards(): pl.pallas_call(functools.partial(kernel, sizes), out_shape=(jax.ShapeDtyp...  81.8 us
    pallas_call x1, Pallas kernels, shards(): pl.pallas_call(functools.partial(finish, (owned, KX, C, L)), out_shape=(j...  34.5 us

profile of v1, /device:TPU:0, one launch (start us, length us, event | category | flops | bytes accessed | tf_op | source)
XLA Modules:
  0.0 117.0 jit_solution(9718372693120259672)
XLA Ops:
  0.6 81.8 %shard_map.182 = (f32[4,32,1024]{2,1,0:T(8,128)}, f32[4,32,1024]{2,1,0:T(8,128)}, f32[256,128]{1,0:T(8,128)}, f32[256,128]{1,0:T(8,128)}, f32[32,32]{1,0:T(8,128)}, /*index=5*/f32[1,32]{1,0:T(1,128)}) custom-call(f32[4,32,1024]{2,1,0:T(8,128)} %field.1, f32[4,32,1024]{2,1,0:T(8,128)} %cotangent.1, f32[4,32,2,32,128]{4,3,2,1,0:T(8,128)} %weight_in.1, ...), custom_call_target="tpu_custom_call" | custom-call | tf_op jit(solution)/shard_map/pallas_call | solution.py:466
  82.5 34.5 %shard_map.183 = (f32[4,32,1024]{2,1,0:T(8,128)}, f32[4,32,1024]{2,1,0:T(8,128)}, f32[4,32,2,32,128]{4,3,2,1,0:T(8,128)}, f32[32,32]{1,0:T(8,128)}, f32[1,32]{1,0:T(1,128)}) custom-call(f32[256,128]{1,0:T(8,128)} %get-tuple-element.16.spectrum, f32[256,128]{1,0:T(8,128)} %get-tuple-element.17.slopes, f32[4,32,1024]{2,1,0:T(8,128)} %get-tuple-element.18.output_in, ...), custom_call_target="tpu_custom_call" | custom-call | tf_op jit(solution)/shard_map/pallas_call | solution.py:506

commit v2 on v1

--- a/solution.py
+++ b/solution.py
@@ -130,12 +130,9 @@
     output, grad_field, grad_weight_out, grad_point, grad_bias, grad_weight, sem,
 ):
     owned, KX, C, L = sizes
-    copies = [
-        pltpu.make_async_copy(output_in, output, sem.at[owned]),
-        pltpu.make_async_copy(field_in, grad_field, sem.at[owned + 1]),
-    ]
-    for copy in copies:
-        copy.start()
+    copies = []
+    output[...] = output_in[...]
+    grad_field[...] = field_in[...]
     grad_point[...] = point_in[...]
     grad_bias[...] = bias_in[...]
     pick, group = channel_tables(C, L)
@@ -512,9 +509,9 @@
             jax.ShapeDtypeStruct((C, C), F32),
             jax.ShapeDtypeStruct((1, C), F32),
         ),
-        in_specs=[vmem, vmem, far, far, vmem, vmem],
-        out_specs=(far, far, far, vmem, vmem),
-        scratch_shapes=[pltpu.VMEM(weight.shape, F32), dma((owned + 2,))],
+        in_specs=[vmem] * 6,
+        out_specs=(vmem, vmem, far, vmem, vmem),
+        scratch_shapes=[pltpu.VMEM(weight.shape, F32), dma((owned,))],
         compiler_params=pltpu.CompilerParams(vmem_limit_bytes=VMEM_BYTES),
     )(spectrum, slopes, output, grad_field, grad_point, grad_bias)
     return (*results[:4], results[4].reshape(C))

time: 117 us -> 87.5 us (0.75)
  Pallas kernels: 116 us -> 86.7 us
    pallas_call x1, Pallas kernels: 34.5 us -> 4.88 us  [shards(): pl.pallas_call(functools.partial(finish, (owned, KX, C, L)), out_shape=(j...]
where the time goes in v2:
time: 87.5 us; the launch traced here: 87.4 us
  Pallas kernels  86.7 us (99%)
    pallas_call x1, Pallas kernels, shards(): pl.pallas_call(functools.partial(kernel, sizes), out_shape=(jax.ShapeDtyp...  81.8 us
    pallas_call x1, Pallas kernels, shards(): pl.pallas_call(functools.partial(finish, (owned, KX, C, L)), out_shape=(j...  4.88 us

profile of v2, /device:TPU:0, one launch (start us, length us, event | category | flops | bytes accessed | tf_op | source)
XLA Modules:
  0.0 87.4 jit_solution(9504570664940520197)
XLA Ops:
  0.6 81.8 %shard_map.182 = (f32[4,32,1024]{2,1,0:T(8,128)}, f32[4,32,1024]{2,1,0:T(8,128)}, f32[256,128]{1,0:T(8,128)}, f32[256,128]{1,0:T(8,128)}, f32[32,32]{1,0:T(8,128)}, /*index=5*/f32[1,32]{1,0:T(1,128)}) custom-call(f32[4,32,1024]{2,1,0:T(8,128)} %field.1, f32[4,32,1024]{2,1,0:T(8,128)} %cotangent.1, f32[4,32,2,32,128]{4,3,2,1,0:T(8,128)} %weight_in.1, ...), custom_call_target="tpu_custom_call" | custom-call | tf_op jit(solution)/shard_map/pallas_call | solution.py:463
  82.5 4.9 %shard_map.183 = (f32[4,32,1024]{2,1,0:T(8,128)}, f32[4,32,1024]{2,1,0:T(8,128)}, f32[4,32,2,32,128]{4,3,2,1,0:T(8,128)}, f32[32,32]{1,0:T(8,128)}, f32[1,32]{1,0:T(1,128)}) custom-call(f32[256,128]{1,0:T(8,128)} %get-tuple-element.16.spectrum, f32[256,128]{1,0:T(8,128)} %get-tuple-element.17.slopes, f32[4,32,1024]{2,1,0:T(8,128)} %get-tuple-element.18.output_in, ...), custom_call_target="tpu_custom_call" | custom-call | tf_op jit(solution)/shard_map/pallas_call | solution.py:503
